TPU v7x, 32 devices: a whole 2x2x4 slice. The times are simulated.
32 devices in a mesh: lat: 4 (over z), lon: 4 (over y, core), buf: 2 (over x).
Axes of the slice: x: 2, y: 2, z: 4, core: 2. Of those that a mesh axis runs over, the one named last changes fastest.
Arguments:
- store: bfloat16 [8, 64, 64, 1725], P('buf', ('lat', 'lon')), may hold values from -6 to 6
- sample_index: int32 [6], replicated, may hold values from 0 to 7, as said below
- region_ids: int32 [64, 64], replicated, may hold values from 0 to 2
- w_embed: bfloat16 [1725, 512], replicated, may hold values from -0.15625 to 0.15625
- attn_gain: float32 [512], replicated, may hold values from 0.1 to 1.9
- w_qkv: bfloat16 [512, 1536], replicated, may hold values from -8 to 8
- w_out: bfloat16 [512, 512], replicated, may hold values from -0.25 to 0.25
- out_gain: float32 [512], replicated, may hold values from 0.1 to 1.9
- w_dec: bfloat16 [512, 1725], replicated, may hold values from -0.25 to 0.25
Outputs:
- new_store: bfloat16 [8, 64, 64, 1725], P('buf', ('lat', 'lon'))
Inputs may be any that keep to these rules, and one draw needn't show every extreme that they name: `sample_index`: distinct slot numbers.
All inputs are finite; a program needn't handle non-finite values.
Results may differ from a plain program's by a relative error of at most 0.007.
Values may be sent and summed in bfloat16 or wider, within the bound.
A program may use at most 128 MiB of HBM per device.

v0:
```python
import math
import jax
import jax.numpy as jnp
from jax import lax
from jax.sharding import PartitionSpec as P

D = 512
HEADS = 8
HDIM = 64
WIN = 8


def with_halo(array, sides, width):
    for axis, dim in sides:
        devices, length = (lax.axis_size(axis), array.shape[dim])
        up = [(i, (i + 1) % devices) for i in range(devices)]
        down = [(j, i) for i, j in up]
        last = lax.slice_in_dim(array, length - width, length, axis=dim)
        leading = lax.slice_in_dim(array, 0, width, axis=dim)
        before = lax.ppermute(last, axis, up)
        after = lax.ppermute(leading, axis, down)
        array = jnp.concatenate([before, array, after], axis=dim)
    return array


def layer_norm(values, gain_row):
    center = jnp.mean(values, axis=-1, keepdims=True)
    spread = jnp.mean(jnp.square(values - center), axis=-1, keepdims=True)
    return (values - center) * lax.rsqrt(spread + 1e-05) * gain_row


def window_mix(windows, regions):
    scores = jnp.einsum(
        "bwqhd,bwkhd->bwhqk",
        windows[:, :, :, 0],
        windows[:, :, :, 1],
        preferred_element_type=jnp.float32,
    ) / math.sqrt(HDIM)
    visible = (regions[:, :, None] == regions[:, None, :])[None, :, None]
    scores = jnp.where(visible, scores, -1e30)
    highest = jnp.max(scores, axis=-1, keepdims=True)
    expo_terms = jnp.where(visible, jnp.exp(scores - highest), 0.0)
    weights = (expo_terms / jnp.sum(expo_terms, axis=-1, keepdims=True)).astype(jnp.bfloat16)
    return jnp.einsum(
        "bwhqk,bwkhd->bwqhd", weights, windows[:, :, :, 2], preferred_element_type=jnp.float32
    ).astype(jnp.bfloat16)


def local(store, sample_index, region_ids, w_embed, attn_gain, w_qkv, w_out, out_gain, w_dec):
    lon_count = lax.axis_size("lon")
    slots_here, rows_here, width_all, patch_len = store.shape
    patch_cols = width_all // lon_count
    patch_rows = rows_here * lon_count
    half_win = WIN // 2
    ext_rows = patch_rows + WIN
    ext_cols = patch_cols + WIN
    own_slots = lax.axis_index("buf") * slots_here + jnp.arange(slots_here, dtype=jnp.int32)
    matches = own_slots[:, None] == sample_index[None, :]
    occupied = jnp.any(matches, axis=1)
    local_rows = store.reshape(slots_here, 1, rows_here, lon_count, patch_cols, patch_len)
    tile_data = lax.all_to_all(local_rows, "lon", split_axis=3, concat_axis=1, tiled=True)
    patches = tile_data.reshape(-1, patch_len)
    embedded = jnp.dot(patches, w_embed, preferred_element_type=jnp.float32).astype(jnp.bfloat16)
    normed = layer_norm(embedded.astype(jnp.float32), attn_gain).astype(jnp.bfloat16)
    normed = normed.reshape(slots_here, patch_rows, patch_cols, D)
    widened = with_halo(normed, (("lat", 1), ("lon", 2)), half_win)
    projected = jnp.dot(widened.reshape(-1, D), w_qkv, preferred_element_type=jnp.float32).astype(
        jnp.bfloat16
    )
    windows = projected.reshape(
        slots_here, ext_rows // WIN, WIN, ext_cols // WIN, WIN, 3, HEADS, HDIM
    )
    windows = windows.transpose(0, 1, 3, 2, 4, 5, 6, 7).reshape(
        slots_here, -1, WIN * WIN, 3, HEADS, HDIM
    )
    total_rows, total_cols = region_ids.shape
    row_pick = (
        lax.axis_index("lat") * patch_rows - half_win + jnp.arange(ext_rows, dtype=jnp.int32)
    ) % total_rows
    col_pick = (
        lax.axis_index("lon") * patch_cols - half_win + jnp.arange(ext_cols, dtype=jnp.int32)
    ) % total_cols
    local_regions = jnp.take(jnp.take(region_ids, row_pick, axis=0), col_pick, axis=1)
    region_windows = (
        local_regions.reshape(ext_rows // WIN, WIN, ext_cols // WIN, WIN)
        .transpose(0, 2, 1, 3)
        .reshape(-1, WIN * WIN)
    )
    mixed_heads = window_mix(windows, region_windows)
    placed = mixed_heads.reshape(slots_here, ext_rows // WIN, ext_cols // WIN, WIN, WIN, D)
    placed = placed.transpose(0, 1, 3, 2, 4, 5).reshape(slots_here, ext_rows, ext_cols, D)
    placed = placed[:, half_win : half_win + patch_rows, half_win : half_win + patch_cols].reshape(
        -1, D
    )
    updated = embedded.astype(jnp.float32) + jnp.dot(
        placed, w_out, preferred_element_type=jnp.float32
    )
    final_norm = layer_norm(updated, out_gain).astype(jnp.bfloat16)
    predicted = (
        patches.astype(jnp.float32) + jnp.dot(final_norm, w_dec, preferred_element_type=jnp.float32)
    ).astype(jnp.bfloat16)
    outgoing = predicted.reshape(slots_here, lon_count, rows_here, 1, patch_cols, patch_len)
    returned = lax.all_to_all(outgoing, "lon", split_axis=1, concat_axis=3, tiled=True)
    strip_data = returned.reshape(slots_here, rows_here, width_all, patch_len)
    return jnp.where(occupied[:, None, None, None], strip_data, store)


def solution(mesh):
    return jax.shard_map(
        local,
        mesh=mesh,
        in_specs=(P("buf", ("lat", "lon"), None, None), P(), P(), P(), P(), P(), P(), P(), P()),
        out_specs=P("buf", ("lat", "lon"), None, None),
        check_vma=False,
    )
```

profile of v0, /device:TPU:0, one launch (start us, length us, event | category | flops | bytes accessed | tf_op | source)
XLA Modules:
  0.0 231.9 jit_solution(15052900297631613152)
XLA Ops:
  0.0 4.4 %copy.71 = bf16[4,1,4,4,16,1725]{5,4,2,0,1,3:T(8,128)(2,1)} copy(bf16[4,1,4,4,16,1725]{5,4,3,2,0,1:T(8,128)(2,1)} %bitcast.55) | data formatting | bytes 7065600 | tf_op jit(solution)/shard_map/reshape | solution.py:60
  4.4 4.9 %all-to-all-start = ((bf16[4,1,4,4,16,1725]{5,4,2,0,1,3:T(8,128)(2,1)}), bf16[4,1,4,4,16,1725]{5,4,2,0,1,3:T(8,128)(2,1)}, u32[]{:S(2)}, u32[]{:S(2)}) async-start(bf16[4,1,4,4,16,1725]{5,4,2,0,1,3:T(8,128)(2,1)} %copy.71), calls=%async_computation | async-start | bytes 7340032 | tf_op jit(solution)/shard_map/all_to_all | solution.py:61
  9.4 0.6 gather_fusion
  10.0 0.1 broadcast_select_fusion.1
  10.0 42.5 %all-to-all-done = bf16[4,1,4,4,16,1725]{5,4,2,0,1,3:T(8,128)(2,1)} async-done(((bf16[4,1,4,4,16,1725]{5,4,2,0,1,3:T(8,128)(2,1)}), bf16[4,1,4,4,16,1725]{5,4,2,0,1,3:T(8,128)(2,1)}, u32[]{:S(2)}, u32[]{:S(2)}) %all-to-all-start) | async-done | bytes 3532832 | tf_op jit(solution)/shard_map/all_to_all | solution.py:61
  52.6 2.4 %copy.72 = bf16[4,4,1,4,1,16,1725]{6,5,3,1,0,4,2:T(8,128)(2,1)S(1)} copy(bf16[4,4,1,4,1,16,1725]{6,5,3,0,1,4,2:T(8,128)(2,1)} %bitcast.2) | data formatting | bytes 7065600 | tf_op jit(solution)/shard_map/all_to_all | solution.py:61
  55.0 0.2 copy-done.9
  55.1 2.1 convert_reduce_fusion
  57.3 0.5 fusion.10
  57.8 0.4 copy-done.3
  58.3 0.4 fusion.12
  58.7 0.8 fusion.24
  59.5 2.4 %collective-permute-start = (bf16[4,4,16,512]{3,2,1,0:T(8,128)(2,1)}, bf16[4,4,16,512]{3,2,1,0:T(8,128)(2,1)S(1)}, u32[]{:S(2)}, u32[]{:S(2)}) collective-permute-start(bf16[4,4,16,512]{3,2,1,0:T(8,128)(2,1)} %get-tuple-element.7), channel_id=1, source_target_pairs={{0,8},{8,16},{16,24},{24,0},{1,9},{9,17},{17,25},{25,1},{2,10},{10... | collective-permute-start | bytes 786440 | tf_op jit(solution)/shard_map/ppermute | solution.py:20
  61.9 2.0 collective-permute-start.1
  64.0 0.1 copy.75
  64.1 0.6 gather_fusion.1
  64.7 0.1 gather.12
  64.8 6.6 %collective-permute-done = bf16[4,4,16,512]{3,2,1,0:T(8,128)(2,1)S(1)} collective-permute-done((bf16[4,4,16,512]{3,2,1,0:T(8,128)(2,1)}, bf16[4,4,16,512]{3,2,1,0:T(8,128)(2,1)S(1)}, u32[]{:S(2)}, u32[]{:S(2)}) %collective-permute-start) | collective-permute-done | bytes 262176 | tf_op jit(solution)/shard_map/ppermute | solution.py:20
  71.4 3.9 %collective-permute-done.1 = bf16[4,4,16,512]{3,2,1,0:T(8,128)(2,1)S(1)} collective-permute-done((bf16[4,4,16,512]{3,2,1,0:T(8,128)(2,1)}, bf16[4,4,16,512]{3,2,1,0:T(8,128)(2,1)S(1)}, u32[]{:S(2)}, u32[]{:S(2)}) %collective-permute-start.1) | collective-permute-done | bytes 262176 | tf_op jit(solution)/shard_map/ppermute | solution.py:21
  75.3 1.2 pad_maximum_fusion.3
  76.5 1.7 collective-permute-start.3
  78.3 0.1 eq.38
  78.4 0.2 broadcast_compare_fusion
  78.5 5.9 %copy.73 = bf16[1024,1725]{0,1:T(8,128)(2,1)} copy(bf16[1024,1725]{1,0:T(8,128)(2,1)} %bitcast.53) | data formatting | bytes 7065600 | tf_op jit(solution)/shard_map/reshape | solution.py:62
  84.5 2.9 %collective-permute-done.2 = bf16[4,24,4,512]{3,2,1,0:T(4,128)(2,1)} collective-permute-done((bf16[4,24,4,512]{3,2,1,0:T(4,128)(2,1)}, bf16[4,24,4,512]{3,2,1,0:T(4,128)(2,1)}, u32[]{:S(2)}, u32[]{:S(2)}) %collective-permute-start.2) | collective-permute-done | bytes 393248 | tf_op jit(solution)/shard_map/ppermute | solution.py:20
  87.4 2.8 %pad_maximum_fusion = bf16[4,24,24,512]{3,2,1,0:T(8,128)(2,1)S(1)} fusion(bf16[4,24,4,512]{3,2,1,0:T(4,128)(2,1)} %collective-permute-done.3, bf16[4,4,16,512]{3,2,1,0:T(8,128)(2,1)S(1)} %collective-permute-done.1, bf16[4,16,16,512]{3,2,1,0:T(8,128)(2,1)S(1)} %bitcast.59, bf16[4,4,16,512]{3,2,1,0:T(8,128)(2,1)S(1)} %collective-permute-done, ...), kind=kLoop, calls=%fused_computation.25 | loop fusion | flops 11796480 | bytes 4718592 | tf_op jit(solution)/shard_map/concatenate | solution.py:22
  90.2 5.8 %convolution_convert_fusion = bf16[2304,1536]{1,0:T(8,128)(2,1)} fusion(bf16[2304,512]{1,0:T(8,128)(2,1)S(1)} %bitcast.63, bf16[512,1536]{1,0:T(8,128)(2,1)S(1)} %copy-done.10), kind=kOutput, calls=%fused_computation.3 | convolution fusion | flops 3627417600 | bytes 11010048 | tf_op jit(solution)/shard_map/dot_general | solution.py:67
  96.0 18.0 %reshape.191 = bf16[4,3,8,3,8,3,8,64]{7,6,5,4,3,2,1,0:T(8,128)(2,1)} reshape(bf16[2304,1536]{1,0:T(8,128)(2,1)} %convolution_convert_fusion) | data formatting | bytes 14155776 | tf_op jit(solution)/shard_map/reshape | solution.py:70
  114.0 11.2 %copy.74 = bf16[4,3,3,8,8,3,8,64]{7,4,3,6,2,1,0,5:T(8,128)(2,1)} copy(bf16[4,3,3,8,8,3,8,64]{7,6,5,4,2,3,1,0:T(8,128)(2,1)} %bitcast.51) | data formatting | bytes 14155776 | tf_op jit(solution)/shard_map/transpose | solution.py:73
  125.2 6.4 %fusion.3 = f32[4,9,8,64,64]{3,4,2,1,0:T(8,128)S(1)} fusion(bf16[4,9,64,3,8,64]{5,2,4,1,0,3:T(8,128)(2,1)} %bitcast.49), kind=kOutput, calls=%fused_computation.11 | convolution fusion | flops 150994944 | bytes 14155776 | tf_op jit(solution)/shard_map/bwqhd,bwkhd->bwhqk/dot_general | solution.py:33
  131.6 5.4 %fusion.25 = (f32[4,9,8,64]{3,2,1,0:T(8,128)S(1)}, f32[4,9,8,64,64]{3,4,2,1,0:T(8,128)}) fusion(f32[4,9,8,64,64]{3,4,2,1,0:T(8,128)S(1)} %fusion.3, pred[9,64,64]{1,2,0:T(8,128)(4,1)S(1)} %broadcast_compare_fusion), kind=kOutput, calls=%fused_computation.76 | output fusion | flops 8257599 | bytes 9547776 | tf_op jit(solution)/shard_map/sub | solution.py:42
  137.0 9.2 %convert_bitcast_fusion = bf16[4,9,64,8,64]{2,4,3,1,0:T(8,128)(2,1)} fusion(f32[4,9,8,64,64]{3,4,2,1,0:T(8,128)} %get-tuple-element.12, f32[4,9,8,64]{3,2,1,0:T(8,128)S(1)} %get-tuple-element.11, bf16[4,9,64,3,8,64]{5,2,4,1,0,3:T(8,128)(2,1)} %bitcast.50), kind=kOutput, calls=%fused_computation.14 | convolution fusion | flops 154533888 | bytes 16588800 | tf_op jit(solution)/shard_map/bwhqk,bwkhd->bwqhd/dot_general | solution.py:44
  146.2 7.0 %copy.80 = bf16[4,9,64,8,64]{4,3,2,1,0:T(8,128)(2,1)} copy(bf16[4,9,64,8,64]{2,4,3,1,0:T(8,128)(2,1)} %convert_bitcast_fusion) | data formatting | bytes 4718592 | tf_op jit(solution)/shard_map/convert_element_type | solution.py:46
  153.1 7.4 %reshape.193 = bf16[4,3,3,8,8,512]{5,4,3,2,1,0:T(8,128)(2,1)} reshape(bf16[4,9,64,8,64]{4,3,2,1,0:T(8,128)(2,1)} %copy.80) | data formatting | bytes 4718592 | tf_op jit(solution)/shard_map/reshape | solution.py:90
  160.5 1.9 copy.81
  162.4 0.5 slice.41
  163.0 0.8 fusion.26
  163.8 0.4 multiply_reduce_fusion
  164.2 0.7 copy-done.5
  164.9 4.1 %add_convert_fusion = bf16[1024,1725]{0,1:T(8,128)(2,1)} fusion(bf16[1024,1725]{0,1:T(8,128)(2,1)S(1)} %copy-done.5, bf16[512,1725]{0,1:T(8,128)(2,1)S(1)} %copy-done, f32[1024,512]{1,0:T(8,128)S(1)} %get-tuple-element.14, f32[512]{0:T(512)S(1)} %copy-done.11, f32[1024]{0:T(1024)S(1)} %add_rsqrt_fusion, f32[1024]{0:T(1024)S(1)} %broadcast_multiply_fusion), kind=kOutput, calls=%fused_computation.8 | convolution fusion | flops 1816189952 | bytes 10939392 | tf_op jit(solution)/shard_map/dot_general | solution.py:100
  169.0 5.8 %copy.83 = bf16[1024,1725]{1,0:T(8,128)(2,1)} copy(bf16[1024,1725]{0,1:T(8,128)(2,1)} %add_convert_fusion) | data formatting | bytes 7065600 | tf_op jit(solution)/shard_map/convert_element_type | solution.py:101
  174.8 4.2 %copy.84 = bf16[4,4,4,1,16,1725]{5,4,2,0,3,1:T(8,128)(2,1)} copy(bf16[4,4,4,1,16,1725]{5,4,2,1,0,3:T(8,128)(2,1)} %bitcast.54) | data formatting | bytes 7065600 | tf_op jit(solution)/shard_map/reshape | solution.py:102
  179.0 4.9 %all-to-all-start.1 = ((bf16[4,4,4,1,16,1725]{5,4,2,0,3,1:T(8,128)(2,1)}), bf16[4,4,4,1,16,1725]{5,4,2,0,3,1:T(8,128)(2,1)}, u32[]{:S(2)}, u32[]{:S(2)}) async-start(bf16[4,4,4,1,16,1725]{5,4,2,0,3,1:T(8,128)(2,1)} %copy.84), calls=%async_computation.1 | async-start | bytes 7340032 | tf_op jit(solution)/shard_map/all_to_all | solution.py:103
  183.9 0.2 compare_reduce_fusion
  184.1 42.4 %all-to-all-done.1 = bf16[4,4,4,1,16,1725]{5,4,2,0,3,1:T(8,128)(2,1)} async-done(((bf16[4,4,4,1,16,1725]{5,4,2,0,3,1:T(8,128)(2,1)}), bf16[4,4,4,1,16,1725]{5,4,2,0,3,1:T(8,128)(2,1)}, u32[]{:S(2)}, u32[]{:S(2)}) %all-to-all-start.1) | async-done | bytes 3532832 | tf_op jit(solution)/shard_map/all_to_all | solution.py:103
  226.5 2.6 %copy.85 = bf16[4,4,4,1,16,1725]{5,4,1,2,0,3:T(8,128)(2,1)S(1)} copy(bf16[4,4,4,1,16,1725]{5,4,2,0,3,1:T(8,128)(2,1)} %all-to-all-done.1) | data formatting | bytes 7065600 | tf_op jit(solution)/shard_map/all_to_all | solution.py:103
  229.2 0.5 copy-done.2
  229.7 2.3 broadcast_select_fusion
  (38 shorter events, 0.2 us)
Async XLA Ops:
  0.0 164.2 %copy-start = (bf16[512,1725]{0,1:T(8,128)(2,1)S(1)}, bf16[512,1725]{0,1:T(8,128)(2,1)}, u32[]{:S(2)}) copy-start(bf16[512,1725]{0,1:T(8,128)(2,1)} %param.17) | copy-start | bytes 5299204
  4.4 4.9 %copy-start.7 = (s32[64,64]{1,0:T(8,128)S(1)}, s32[64,64]{1,0:T(8,128)}, u32[]{:S(2)}) copy-start(s32[64,64]{1,0:T(8,128)} %param.11) | copy-start | bytes 49156
  4.4 48.1 %all-to-all-start = ((bf16[4,1,4,4,16,1725]{5,4,2,0,1,3:T(8,128)(2,1)}), bf16[4,1,4,4,16,1725]{5,4,2,0,1,3:T(8,128)(2,1)}, u32[]{:S(2)}, u32[]{:S(2)}) async-start(bf16[4,1,4,4,16,1725]{5,4,2,0,1,3:T(8,128)(2,1)} %copy.71), calls=%async_computation | async-start | bytes 7340032 | tf_op jit(solution)/shard_map/all_to_all | solution.py:61
  52.6 2.6 %copy-start.9 = (bf16[1725,512]{1,0:T(8,128)(2,1)S(1)}, bf16[1725,512]{1,0:T(8,128)(2,1)}, u32[]{:S(2)}) copy-start(bf16[1725,512]{1,0:T(8,128)(2,1)} %param.12) | copy-start | bytes 5299204
  55.0 2.3 copy-start.1
  55.1 3.1 %copy-start.8 = (f32[512]{0:T(512)S(1)}, f32[512]{0:T(512)}, u32[]{:S(2)}) copy-start(f32[512]{0:T(512)} %param.13) | copy-start | bytes 6148
  57.3 1.0 copy-start.3
  59.5 11.8 %collective-permute-start = (bf16[4,4,16,512]{3,2,1,0:T(8,128)(2,1)}, bf16[4,4,16,512]{3,2,1,0:T(8,128)(2,1)S(1)}, u32[]{:S(2)}, u32[]{:S(2)}) collective-permute-start(bf16[4,4,16,512]{3,2,1,0:T(8,128)(2,1)} %get-tuple-element.7), channel_id=1, source_target_pairs={{0,8},{8,16},{16,24},{24,0},{1,9},{9,17},{17,25},{25,1},{2,10},{10... | collective-permute-start | bytes 786440 | tf_op jit(solution)/shard_map/ppermute | solution.py:20
  61.9 13.4 %collective-permute-start.1 = (bf16[4,4,16,512]{3,2,1,0:T(8,128)(2,1)}, bf16[4,4,16,512]{3,2,1,0:T(8,128)(2,1)S(1)}, u32[]{:S(2)}, u32[]{:S(2)}) collective-permute-start(bf16[4,4,16,512]{3,2,1,0:T(8,128)(2,1)} %get-tuple-element.8), channel_id=1, source_target_pairs={{8,0},{16,8},{24,16},{0,24},{9,1},{17,9},{25,17},{1,25},{10,2},{18... | collective-permute-start | bytes 786440 | tf_op jit(solution)/shard_map/ppermute | solution.py:21
  76.5 10.8 %collective-permute-start.2 = (bf16[4,24,4,512]{3,2,1,0:T(4,128)(2,1)}, bf16[4,24,4,512]{3,2,1,0:T(4,128)(2,1)}, u32[]{:S(2)}, u32[]{:S(2)}) collective-permute-start(bf16[4,24,4,512]{3,2,1,0:T(4,128)(2,1)} %get-tuple-element.5), channel_id=1, source_target_pairs={{0,2},{2,4},{4,6},{6,0},{1,3},{3,5},{5,7},{7,1},{8,10},{10,12},{12... | collective-permute-start | bytes 1179656 | tf_op jit(solution)/shard_map/ppermute | solution.py:20
  76.5 10.8 %collective-permute-start.3 = (bf16[4,24,4,512]{3,2,1,0:T(4,128)(2,1)}, bf16[4,24,4,512]{3,2,1,0:T(4,128)(2,1)}, u32[]{:S(2)}, u32[]{:S(2)}) collective-permute-start(bf16[4,24,4,512]{3,2,1,0:T(4,128)(2,1)} %get-tuple-element.6), channel_id=1, source_target_pairs={{2,0},{4,2},{6,4},{0,6},{3,1},{5,3},{7,5},{1,7},{10,8},{12,10},{14... | collective-permute-start | bytes 1179656 | tf_op jit(solution)/shard_map/ppermute | solution.py:21
  84.5 5.7 %copy-start.10 = (bf16[512,1536]{1,0:T(8,128)(2,1)S(1)}, bf16[512,1536]{1,0:T(8,128)(2,1)}, u32[]{:S(2)}) copy-start(bf16[512,1536]{1,0:T(8,128)(2,1)} %param.14) | copy-start | bytes 4718596
  160.5 2.5 %copy-start.4 = (bf16[1024,512]{1,0:T(8,128)(2,1)S(1)}, bf16[1024,512]{1,0:T(8,128)(2,1)}, u32[]{:S(2)}) copy-start(bf16[1024,512]{1,0:T(8,128)(2,1)} %copy-done.3) | copy-start | bytes 3145732
  160.5 2.5 %copy-start.6 = (bf16[512,512]{1,0:T(8,128)(2,1)S(1)}, bf16[512,512]{1,0:T(8,128)(2,1)}, u32[]{:S(2)}) copy-start(bf16[512,512]{1,0:T(8,128)(2,1)} %param.15) | copy-start | bytes 1572868
  162.9 2.0 copy-start.5
  162.9 2.0 copy-start.11
  179.0 4.9 %copy-start.12 = (s32[6]{0:T(128)S(1)}, s32[6]{0:T(128)}, u32[]{:S(2)}) copy-start(s32[6]{0:T(128)} %param.10) | copy-start | bytes 76
  179.0 47.5 %all-to-all-start.1 = ((bf16[4,4,4,1,16,1725]{5,4,2,0,3,1:T(8,128)(2,1)}), bf16[4,4,4,1,16,1725]{5,4,2,0,3,1:T(8,128)(2,1)}, u32[]{:S(2)}, u32[]{:S(2)}) async-start(bf16[4,4,4,1,16,1725]{5,4,2,0,3,1:T(8,128)(2,1)} %copy.84), calls=%async_computation.1 | async-start | bytes 7340032 | tf_op jit(solution)/shard_map/all_to_all | solution.py:103
  226.5 3.1 %copy-start.2 = (bf16[4,4,64,1725]{3,2,1,0:T(8,128)(2,1)S(1)}, bf16[4,4,64,1725]{3,2,1,0:T(8,128)(2,1)}, u32[]{:S(2)}) copy-start(bf16[4,4,64,1725]{3,2,1,0:T(8,128)(2,1)} %param.9) | copy-start | bytes 10598404
where the time goes:
time: 233 us; the launch traced here: 232 us
  waiting for transfers between devices  98.3 us (42%)
  local copies, waits for them, and re-layouts  75.5 us (32%)
  matrix products  28.4 us (12%)
  starting transfers between devices  15.9 us (7%)
  other arithmetic  13.5 us (6%)
    all_to_all x1, waiting for transfers between devices, local(): lax.all_to_all(local_rows, 'lon', split_axis=3, concat_axis=1, tiled=True)  42.5 us
    all_to_all x1, waiting for transfers between devices, local(): lax.all_to_all(outgoing, 'lon', split_axis=1, concat_axis=3, tiled=True)  42.4 us
    reshape x1, local copies, waits for them, and re-layouts, local(): projected.reshape(slots_here, ext_rows // WIN, WIN, ext_cols // WIN, WIN,...  18 us
    transpose x1, local copies, waits for them, and re-layouts, local(): windows.transpose(0, 1, 3, 2, 4, 5, 6, 7)  11.2 us
    ppermute x2, waiting for transfers between devices, with_halo(): before = lax.ppermute(last, axis, up)  9.45 us
    dot_general x1, matrix products, window_mix(): jnp.einsum('bwhqk,bwkhd->bwqhd', weights, windows[:, :, :, 2], preferred_...  9.19 us
    reshape x1, local copies, waits for them, and re-layouts, local(): mixed_heads.reshape(slots_here, ext_rows // WIN, ext_cols // WIN, WIN, WI...  7.36 us
    convert_element_type x1, local copies, waits for them, and re-layouts, window_mix(): return jnp.einsum('bwhqk,bwkhd->bwqhd', weights, windows[:, :, :, 2], pre...  6.99 us
  transfers between devices with their start and end apart: 6, of which 5 were waited for; matrix products, arithmetic and copies ran while one was open for 3% of the time, Pallas kernels for 0%

commit v1 on v0

--- a/solution.py
+++ b/solution.py
@@ -100,7 +100,9 @@
         patches.astype(jnp.float32) + jnp.dot(final_norm, w_dec, preferred_element_type=jnp.float32)
     ).astype(jnp.bfloat16)
     outgoing = predicted.reshape(slots_here, lon_count, rows_here, 1, patch_cols, patch_len)
-    returned = lax.all_to_all(outgoing, "lon", split_axis=1, concat_axis=3, tiled=True)
+    pieces = jnp.split(outgoing, lax.axis_size("lon"), axis=1)
+    received = lax.all_to_all(jnp.stack(pieces), "lon", 0, 0)
+    returned = jnp.concatenate(received, axis=3)
     strip_data = returned.reshape(slots_here, rows_here, width_all, patch_len)
     return jnp.where(occupied[:, None, None, None], strip_data, store)
 

time: 233 us -> 233 us (level)
    all_to_all x1 -> x0, local copies, waits for them, and re-layouts: 2.64 us -> none  [local(): lax.all_to_all(outgoing, 'lon', split_axis=1, concat_axis=3, tiled=True)]
    another operation x0 -> x1, local copies, waits for them, and re-layouts: none -> 2.33 us  [local(): received = lax.all_to_all(jnp.stack(pieces), 'lon', 0, 0)]
where the time goes in v1:
time: 233 us; the launch traced here: 232 us
  waiting for transfers between devices  98.3 us (42%)
  local copies, waits for them, and re-layouts  73.6 us (32%)
  matrix products  28.4 us (12%)
  starting transfers between devices  16 us (7%)
  other arithmetic  15.6 us (7%)
    all_to_all x1, waiting for transfers between devices, local(): lax.all_to_all(local_rows, 'lon', split_axis=3, concat_axis=1, tiled=True)  42.5 us
    all_to_all x1, waiting for transfers between devices, local(): received = lax.all_to_all(jnp.stack(pieces), 'lon', 0, 0)  42.4 us
    reshape x1, local copies, waits for them, and re-layouts, local(): projected.reshape(slots_here, ext_rows // WIN, WIN, ext_cols // WIN, WIN,...  18 us
    transpose x1, local copies, waits for them, and re-layouts, local(): windows.transpose(0, 1, 3, 2, 4, 5, 6, 7)  11.2 us
    ppermute x2, waiting for transfers between devices, with_halo(): before = lax.ppermute(last, axis, up)  9.42 us
    dot_general x1, matrix products, window_mix(): jnp.einsum('bwhqk,bwkhd->bwqhd', weights, windows[:, :, :, 2], preferred_...  9.2 us
    reshape x1, local copies, waits for them, and re-layouts, local(): mixed_heads.reshape(slots_here, ext_rows // WIN, ext_cols // WIN, WIN, WI...  7.36 us
    convert_element_type x1, local copies, waits for them, and re-layouts, window_mix(): return jnp.einsum('bwhqk,bwkhd->bwqhd', weights, windows[:, :, :, 2], pre...  6.98 us
  transfers between devices with their start and end apart: 6, of which 5 were waited for; matrix products, arithmetic and copies ran while one was open for 3% of the time, Pallas kernels for 0%

profile of v1, /device:TPU:0, one launch (start us, length us, event | category | flops | bytes accessed | tf_op | source)
XLA Modules:
  0.0 232.2 jit_solution(5471091866050364807)
XLA Ops:
  0.0 4.4 %copy.84 = bf16[4,1,4,4,16,1725]{5,4,2,0,1,3:T(8,128)(2,1)} copy(bf16[4,1,4,4,16,1725]{5,4,3,2,0,1:T(8,128)(2,1)} %bitcast.66) | data formatting | bytes 7065600 | tf_op jit(solution)/shard_map/reshape | solution.py:60
  4.4 4.9 %all-to-all-start = ((bf16[4,1,4,4,16,1725]{5,4,2,0,1,3:T(8,128)(2,1)}), bf16[4,1,4,4,16,1725]{5,4,2,0,1,3:T(8,128)(2,1)}, u32[]{:S(2)}, u32[]{:S(2)}) async-start(bf16[4,1,4,4,16,1725]{5,4,2,0,1,3:T(8,128)(2,1)} %copy.84), calls=%async_computation | async-start | bytes 7340032 | tf_op jit(solution)/shard_map/all_to_all | solution.py:61
  9.4 0.6 gather_fusion
  10.0 42.5 %all-to-all-done = bf16[4,1,4,4,16,1725]{5,4,2,0,1,3:T(8,128)(2,1)} async-done(((bf16[4,1,4,4,16,1725]{5,4,2,0,1,3:T(8,128)(2,1)}), bf16[4,1,4,4,16,1725]{5,4,2,0,1,3:T(8,128)(2,1)}, u32[]{:S(2)}, u32[]{:S(2)}) %all-to-all-start) | async-done | bytes 3532832 | tf_op jit(solution)/shard_map/all_to_all | solution.py:61
  52.6 2.4 %copy.85 = bf16[4,4,1,4,1,16,1725]{6,5,3,1,0,4,2:T(8,128)(2,1)S(1)} copy(bf16[4,4,1,4,1,16,1725]{6,5,3,0,1,4,2:T(8,128)(2,1)} %bitcast.2) | data formatting | bytes 7065600 | tf_op jit(solution)/shard_map/all_to_all | solution.py:61
  55.0 0.2 copy-done.9
  55.1 2.1 convert_reduce_fusion
  57.3 0.5 fusion.10
  57.8 0.5 copy-done.3
  58.3 0.4 fusion.12
  58.7 0.8 fusion.24
  59.6 2.4 %collective-permute-start = (bf16[4,4,16,512]{3,2,1,0:T(8,128)(2,1)}, bf16[4,4,16,512]{3,2,1,0:T(8,128)(2,1)S(1)}, u32[]{:S(2)}, u32[]{:S(2)}) collective-permute-start(bf16[4,4,16,512]{3,2,1,0:T(8,128)(2,1)} %get-tuple-element.11), channel_id=1, source_target_pairs={{0,8},{8,16},{16,24},{24,0},{1,9},{9,17},{17,25},{25,1},{2,10},{10... | collective-permute-start | bytes 786440 | tf_op jit(solution)/shard_map/ppermute | solution.py:20
  62.0 2.0 collective-permute-start.1
  64.0 0.1 copy.88
  64.1 0.6 gather_fusion.1
  64.7 0.1 gather.12
  64.9 6.6 %collective-permute-done = bf16[4,4,16,512]{3,2,1,0:T(8,128)(2,1)S(1)} collective-permute-done((bf16[4,4,16,512]{3,2,1,0:T(8,128)(2,1)}, bf16[4,4,16,512]{3,2,1,0:T(8,128)(2,1)S(1)}, u32[]{:S(2)}, u32[]{:S(2)}) %collective-permute-start) | collective-permute-done | bytes 262176 | tf_op jit(solution)/shard_map/ppermute | solution.py:20
  71.4 4.0 %collective-permute-done.1 = bf16[4,4,16,512]{3,2,1,0:T(8,128)(2,1)S(1)} collective-permute-done((bf16[4,4,16,512]{3,2,1,0:T(8,128)(2,1)}, bf16[4,4,16,512]{3,2,1,0:T(8,128)(2,1)S(1)}, u32[]{:S(2)}, u32[]{:S(2)}) %collective-permute-start.1) | collective-permute-done | bytes 262176 | tf_op jit(solution)/shard_map/ppermute | solution.py:21
  75.4 1.2 pad_maximum_fusion.4
  76.6 1.7 collective-permute-start.3
  78.3 0.1 eq.38
  78.4 0.2 broadcast_compare_fusion
  78.6 5.9 %copy.86 = bf16[1024,1725]{0,1:T(8,128)(2,1)} copy(bf16[1024,1725]{1,0:T(8,128)(2,1)} %bitcast.64) | data formatting | bytes 7065600 | tf_op jit(solution)/shard_map/reshape | solution.py:62
  84.5 2.9 %collective-permute-done.2 = bf16[4,24,4,512]{3,2,1,0:T(4,128)(2,1)} collective-permute-done((bf16[4,24,4,512]{3,2,1,0:T(4,128)(2,1)}, bf16[4,24,4,512]{3,2,1,0:T(4,128)(2,1)}, u32[]{:S(2)}, u32[]{:S(2)}) %collective-permute-start.2) | collective-permute-done | bytes 393248 | tf_op jit(solution)/shard_map/ppermute | solution.py:20
  87.4 2.8 %pad_maximum_fusion.1 = bf16[4,24,24,512]{3,2,1,0:T(8,128)(2,1)S(1)} fusion(bf16[4,24,4,512]{3,2,1,0:T(4,128)(2,1)} %collective-permute-done.3, bf16[4,4,16,512]{3,2,1,0:T(8,128)(2,1)S(1)} %collective-permute-done.1, bf16[4,16,16,512]{3,2,1,0:T(8,128)(2,1)S(1)} %bitcast.70, bf16[4,4,16,512]{3,2,1,0:T(8,128)(2,1)S(1)} %collective-permute-done, ...), kind=kLoop, calls=%fused_computation.26 | loop fusion | flops 11796480 | bytes 4718592 | tf_op jit(solution)/shard_map/concatenate | solution.py:22
  90.2 5.8 %convolution_convert_fusion = bf16[2304,1536]{1,0:T(8,128)(2,1)} fusion(bf16[2304,512]{1,0:T(8,128)(2,1)S(1)} %bitcast.74, bf16[512,1536]{1,0:T(8,128)(2,1)S(1)} %copy-done.10), kind=kOutput, calls=%fused_computation.3 | convolution fusion | flops 3627417600 | bytes 11010048 | tf_op jit(solution)/shard_map/dot_general | solution.py:67
  96.0 18.0 %reshape.190 = bf16[4,3,8,3,8,3,8,64]{7,6,5,4,3,2,1,0:T(8,128)(2,1)} reshape(bf16[2304,1536]{1,0:T(8,128)(2,1)} %convolution_convert_fusion) | data formatting | bytes 14155776 | tf_op jit(solution)/shard_map/reshape | solution.py:70
  114.0 11.2 %copy.87 = bf16[4,3,3,8,8,3,8,64]{7,4,3,6,2,1,0,5:T(8,128)(2,1)} copy(bf16[4,3,3,8,8,3,8,64]{7,6,5,4,2,3,1,0:T(8,128)(2,1)} %bitcast.62) | data formatting | bytes 14155776 | tf_op jit(solution)/shard_map/transpose | solution.py:73
  125.2 6.4 %fusion.3 = f32[4,9,8,64,64]{3,4,2,1,0:T(8,128)S(1)} fusion(bf16[4,9,64,3,8,64]{5,2,4,1,0,3:T(8,128)(2,1)} %bitcast.60), kind=kOutput, calls=%fused_computation.11 | convolution fusion | flops 150994944 | bytes 14155776 | tf_op jit(solution)/shard_map/bwqhd,bwkhd->bwhqk/dot_general | solution.py:33
  131.6 5.4 %fusion.25 = (f32[4,9,8,64]{3,2,1,0:T(8,128)S(1)}, f32[4,9,8,64,64]{3,4,2,1,0:T(8,128)}) fusion(f32[4,9,8,64,64]{3,4,2,1,0:T(8,128)S(1)} %fusion.3, pred[9,64,64]{1,2,0:T(8,128)(4,1)S(1)} %broadcast_compare_fusion), kind=kOutput, calls=%fused_computation.81 | output fusion | flops 8257599 | bytes 9547776 | tf_op jit(solution)/shard_map/sub | solution.py:42
  137.0 9.2 %convert_bitcast_fusion = bf16[4,9,64,8,64]{2,4,3,1,0:T(8,128)(2,1)} fusion(f32[4,9,8,64,64]{3,4,2,1,0:T(8,128)} %get-tuple-element.16, f32[4,9,8,64]{3,2,1,0:T(8,128)S(1)} %get-tuple-element.15, bf16[4,9,64,3,8,64]{5,2,4,1,0,3:T(8,128)(2,1)} %bitcast.61), kind=kOutput, calls=%fused_computation.14 | convolution fusion | flops 154533888 | bytes 16588800 | tf_op jit(solution)/shard_map/bwhqk,bwkhd->bwqhd/dot_general | solution.py:44
  146.2 7.0 %copy.93 = bf16[4,9,64,8,64]{4,3,2,1,0:T(8,128)(2,1)} copy(bf16[4,9,64,8,64]{2,4,3,1,0:T(8,128)(2,1)} %convert_bitcast_fusion) | data formatting | bytes 4718592 | tf_op jit(solution)/shard_map/convert_element_type | solution.py:46
  153.2 7.4 %reshape.192 = bf16[4,3,3,8,8,512]{5,4,3,2,1,0:T(8,128)(2,1)} reshape(bf16[4,9,64,8,64]{4,3,2,1,0:T(8,128)(2,1)} %copy.93) | data formatting | bytes 4718592 | tf_op jit(solution)/shard_map/reshape | solution.py:90
  160.5 1.9 copy.94
  162.5 0.5 slice.41
  163.0 0.8 fusion.26
  163.8 0.4 multiply_reduce_fusion
  164.2 0.7 copy-done.5
  165.0 4.1 %add_convert_fusion = bf16[1024,1725]{0,1:T(8,128)(2,1)} fusion(bf16[1024,1725]{0,1:T(8,128)(2,1)S(1)} %copy-done.5, bf16[512,1725]{0,1:T(8,128)(2,1)S(1)} %copy-done, f32[1024,512]{1,0:T(8,128)S(1)} %get-tuple-element.18, f32[512]{0:T(512)S(1)} %copy-done.11, f32[1024]{0:T(1024)S(1)} %add_rsqrt_fusion, f32[1024]{0:T(1024)S(1)} %broadcast_multiply_fusion), kind=kOutput, calls=%fused_computation.8 | convolution fusion | flops 1816189952 | bytes 10939392 | tf_op jit(solution)/shard_map/dot_general | solution.py:100
  169.0 5.8 %copy.96 = bf16[1024,1725]{1,0:T(8,128)(2,1)} copy(bf16[1024,1725]{0,1:T(8,128)(2,1)} %add_convert_fusion) | data formatting | bytes 7065600 | tf_op jit(solution)/shard_map/convert_element_type | solution.py:101
  174.8 2.3 %slice_bitcast_fusion.11 = (bf16[1,4,1,4,1,16,1725]{6,5,3,1,4,2,0:T(8,128)(2,1)S(1)}, bf16[1,4,1,4,1,16,1725]{6,5,3,1,4,2,0:T(8,128)(2,1)S(1)}, bf16[1,4,1,4,1,1...) fusion(bf16[4,4,4,1,16,1725]{5,4,2,1,0,3:T(8,128)(2,1)} %bitcast.65), kind=kLoop, calls=%fused_computation.39 | loop fusion | bytes 7065600 | tf_op jit(solution)/shard_map/stack | solution.py:104
  177.1 2.1 pad_maximum_fusion
  179.2 4.9 %all-to-all-start.1 = ((bf16[4,4,1,4,1,16,1725]{6,5,3,1,4,2,0:T(8,128)(2,1)}), bf16[4,4,1,4,1,16,1725]{6,5,3,1,4,2,0:T(8,128)(2,1)}, u32[]{:S(2)}, u32[]{:S(2)}) async-start(bf16[4,4,1,4,1,16,1725]{6,5,3,1,4,2,0:T(8,128)(2,1)} %pad_maximum_fusion), calls=%async_computation.1 | async-start | bytes 7340032 | tf_op jit(solution)/shard_map/all_to_all | solution.py:104
  184.2 0.2 compare_reduce_fusion
  184.3 42.4 %all-to-all-done.1 = bf16[4,4,1,4,1,16,1725]{6,5,3,1,4,2,0:T(8,128)(2,1)} async-done(((bf16[4,4,1,4,1,16,1725]{6,5,3,1,4,2,0:T(8,128)(2,1)}), bf16[4,4,1,4,1,16,1725]{6,5,3,1,4,2,0:T(8,128)(2,1)}, u32[]{:S(2)}, u32[]{:S(2)}) %all-to-all-start.1) | async-done | bytes 3532832 | tf_op jit(solution)/shard_map/all_to_all | solution.py:104
  226.7 2.6 %copy.100 = bf16[4,1,4,4,1,16,1725]{6,5,3,2,0,4,1:T(8,128)(2,1)S(1)} copy(bf16[4,1,4,4,1,16,1725]{6,5,2,0,4,1,3:T(8,128)(2,1)} %bitcast.24) | data formatting | bytes 7065600 | tf_op jit(solution)/shard_map/reshape | solution.py:105
  229.4 0.5 copy-done.2
  229.9 2.3 broadcast_select_fusion
  (39 shorter events, 0.3 us)
Async XLA Ops:
  0.0 164.2 %copy-start = (bf16[512,1725]{0,1:T(8,128)(2,1)S(1)}, bf16[512,1725]{0,1:T(8,128)(2,1)}, u32[]{:S(2)}) copy-start(bf16[512,1725]{0,1:T(8,128)(2,1)} %param.17) | copy-start | bytes 5299204
  4.4 5.0 %copy-start.7 = (s32[64,64]{1,0:T(8,128)S(1)}, s32[64,64]{1,0:T(8,128)}, u32[]{:S(2)}) copy-start(s32[64,64]{1,0:T(8,128)} %param.11) | copy-start | bytes 49156
  4.4 48.1 %all-to-all-start = ((bf16[4,1,4,4,16,1725]{5,4,2,0,1,3:T(8,128)(2,1)}), bf16[4,1,4,4,16,1725]{5,4,2,0,1,3:T(8,128)(2,1)}, u32[]{:S(2)}, u32[]{:S(2)}) async-start(bf16[4,1,4,4,16,1725]{5,4,2,0,1,3:T(8,128)(2,1)} %copy.84), calls=%async_computation | async-start | bytes 7340032 | tf_op jit(solution)/shard_map/all_to_all | solution.py:61
  52.6 2.6 %copy-start.9 = (bf16[1725,512]{1,0:T(8,128)(2,1)S(1)}, bf16[1725,512]{1,0:T(8,128)(2,1)}, u32[]{:S(2)}) copy-start(bf16[1725,512]{1,0:T(8,128)(2,1)} %param.12) | copy-start | bytes 5299204
  55.0 2.3 copy-start.1
  55.1 3.2 %copy-start.8 = (f32[512]{0:T(512)S(1)}, f32[512]{0:T(512)}, u32[]{:S(2)}) copy-start(f32[512]{0:T(512)} %param.13) | copy-start | bytes 6148
  57.3 1.0 copy-start.3
  59.6 11.9 %collective-permute-start = (bf16[4,4,16,512]{3,2,1,0:T(8,128)(2,1)}, bf16[4,4,16,512]{3,2,1,0:T(8,128)(2,1)S(1)}, u32[]{:S(2)}, u32[]{:S(2)}) collective-permute-start(bf16[4,4,16,512]{3,2,1,0:T(8,128)(2,1)} %get-tuple-element.11), channel_id=1, source_target_pairs={{0,8},{8,16},{16,24},{24,0},{1,9},{9,17},{17,25},{25,1},{2,10},{10... | collective-permute-start | bytes 786440 | tf_op jit(solution)/shard_map/ppermute | solution.py:20
  62.0 13.4 %collective-permute-start.1 = (bf16[4,4,16,512]{3,2,1,0:T(8,128)(2,1)}, bf16[4,4,16,512]{3,2,1,0:T(8,128)(2,1)S(1)}, u32[]{:S(2)}, u32[]{:S(2)}) collective-permute-start(bf16[4,4,16,512]{3,2,1,0:T(8,128)(2,1)} %get-tuple-element.12), channel_id=1, source_target_pairs={{8,0},{16,8},{24,16},{0,24},{9,1},{17,9},{25,17},{1,25},{10,2},{18... | collective-permute-start | bytes 786440 | tf_op jit(solution)/shard_map/ppermute | solution.py:21
  76.6 10.8 %collective-permute-start.2 = (bf16[4,24,4,512]{3,2,1,0:T(4,128)(2,1)}, bf16[4,24,4,512]{3,2,1,0:T(4,128)(2,1)}, u32[]{:S(2)}, u32[]{:S(2)}) collective-permute-start(bf16[4,24,4,512]{3,2,1,0:T(4,128)(2,1)} %get-tuple-element.9), channel_id=1, source_target_pairs={{0,2},{2,4},{4,6},{6,0},{1,3},{3,5},{5,7},{7,1},{8,10},{10,12},{12... | collective-permute-start | bytes 1179656 | tf_op jit(solution)/shard_map/ppermute | solution.py:20
  76.6 10.8 %collective-permute-start.3 = (bf16[4,24,4,512]{3,2,1,0:T(4,128)(2,1)}, bf16[4,24,4,512]{3,2,1,0:T(4,128)(2,1)}, u32[]{:S(2)}, u32[]{:S(2)}) collective-permute-start(bf16[4,24,4,512]{3,2,1,0:T(4,128)(2,1)} %get-tuple-element.10), channel_id=1, source_target_pairs={{2,0},{4,2},{6,4},{0,6},{3,1},{5,3},{7,5},{1,7},{10,8},{12,10},{14... | collective-permute-start | bytes 1179656 | tf_op jit(solution)/shard_map/ppermute | solution.py:21
  84.5 5.7 %copy-start.10 = (bf16[512,1536]{1,0:T(8,128)(2,1)S(1)}, bf16[512,1536]{1,0:T(8,128)(2,1)}, u32[]{:S(2)}) copy-start(bf16[512,1536]{1,0:T(8,128)(2,1)} %param.14) | copy-start | bytes 4718596
  160.5 2.5 %copy-start.4 = (bf16[1024,512]{1,0:T(8,128)(2,1)S(1)}, bf16[1024,512]{1,0:T(8,128)(2,1)}, u32[]{:S(2)}) copy-start(bf16[1024,512]{1,0:T(8,128)(2,1)} %copy-done.3) | copy-start | bytes 3145732
  160.5 2.5 %copy-start.6 = (bf16[512,512]{1,0:T(8,128)(2,1)S(1)}, bf16[512,512]{1,0:T(8,128)(2,1)}, u32[]{:S(2)}) copy-start(bf16[512,512]{1,0:T(8,128)(2,1)} %param.15) | copy-start | bytes 1572868
  162.9 2.0 copy-start.5
  163.0 2.0 copy-start.11
  179.2 4.9 %copy-start.12 = (s32[6]{0:T(128)S(1)}, s32[6]{0:T(128)}, u32[]{:S(2)}) copy-start(s32[6]{0:T(128)} %param.10) | copy-start | bytes 76
  179.2 47.5 %all-to-all-start.1 = ((bf16[4,4,1,4,1,16,1725]{6,5,3,1,4,2,0:T(8,128)(2,1)}), bf16[4,4,1,4,1,16,1725]{6,5,3,1,4,2,0:T(8,128)(2,1)}, u32[]{:S(2)}, u32[]{:S(2)}) async-start(bf16[4,4,1,4,1,16,1725]{6,5,3,1,4,2,0:T(8,128)(2,1)} %pad_maximum_fusion), calls=%async_computation.1 | async-start | bytes 7340032 | tf_op jit(solution)/shard_map/all_to_all | solution.py:104
  226.7 3.1 %copy-start.2 = (bf16[4,4,64,1725]{3,2,1,0:T(8,128)(2,1)S(1)}, bf16[4,4,64,1725]{3,2,1,0:T(8,128)(2,1)}, u32[]{:S(2)}) copy-start(bf16[4,4,64,1725]{3,2,1,0:T(8,128)(2,1)} %param.9) | copy-start | bytes 10598404
